TPU v7x, 512 devices: a whole 4x4x16 slice. The times are simulated.
512 devices in a mesh: seg: 32 (over z, core), sec: 16 (over y, x).
Axes of the slice: x: 4, y: 4, z: 16, core: 2. Of those that a mesh axis runs over, the one named last changes fastest.
Arguments:
- left_env: bfloat16 [32, 16, 16, 256, 256], P('seg', 'sec'), as said below
- right_env: bfloat16 [32, 16, 16, 256, 256], P('seg', 'sec'), as said below
- left_piece: bfloat16 [32, 16, 256, 256], P('seg', 'sec'), may hold values from -0.375 to 0.375
- right_piece: bfloat16 [32, 16, 256, 256], P('seg', 'sec'), may hold values from -0.375 to 0.375
- guess: bfloat16 [32, 16, 256, 256], P('seg', 'sec'), may hold values from -0.375 to 0.375
- inverse_values: float32 [32, 16, 256], P('seg', 'sec'), may hold values from 0.5 to 4
- precond: bfloat16 [32, 16, 256, 256], P('seg', 'sec'), may hold values from 0.25 to 2
- sector_rows: int32 [32, 16], P('seg', 'sec'), may hold values from 64 to 256, as said below
Outputs:
- polar_factor: float32 [32, 16, 256, 256], P('seg', 'sec')
- next_left: bfloat16 [32, 16, 256, 256], P('seg', 'sec')
- energies: float32 [32], P('seg')
Inputs may be any that keep to these rules, and one draw needn't show every extreme that they name: `sector_rows`: some block has 256 live states and some has 64. `left_env`: each channel's block is symmetric. `right_env`: each channel's block is symmetric.
All inputs are finite; a program needn't handle non-finite values.
Results may differ from a plain program's by a relative error of at most 0.006.
Values may be sent and summed in bfloat16 or wider, within the bound.
A program may use at most 64 MiB of HBM per device.

v0:
```python
import jax
import jax.numpy as jnp
from jax import lax
from jax.sharding import PartitionSpec as P

WD = 2
ITERS = 2
NS_STEPS = 3


def from_behind(value, axis, steps):
    count = lax.axis_size(axis)
    first, last = (max(0, -steps), min(count, count - steps))
    return lax.ppermute(value, axis, [(source, source + steps) for source in range(first, last)])


def shards(
    left_env, right_env, left_piece, right_piece, guess, inverse_values, precond, sector_rows
):
    f32 = jnp.float32
    bf16 = jnp.bfloat16
    lenv = left_env[0, 0]
    renv = right_env[0, 0]
    size = lenv.shape[-1]
    count = sector_rows[0, 0]
    idx_r = lax.broadcasted_iota(jnp.int32, (size, size), 0)
    idx_c = lax.broadcasted_iota(jnp.int32, (size, size), 1)
    mask = ((idx_r < count) & (idx_c < count)).astype(f32)
    lraise = lenv[WD:]
    rraise = renv[WD:]

    def lowering(vbf):
        inner = jnp.einsum("wji,jk->wik", lraise, vbf, preferred_element_type=f32).astype(bf16)
        return jnp.einsum("wik,wlk->il", inner, rraise, preferred_element_type=f32).astype(bf16)

    def raising(vbf):
        inner = jnp.einsum("wij,jk->wik", lraise, vbf, preferred_element_type=f32).astype(bf16)
        return jnp.einsum("wik,wkl->il", inner, rraise, preferred_element_type=f32)

    def apply_op(vec):
        vbf = vec.astype(bf16)
        from_below = from_behind(vbf, "sec", 1)
        down = lowering(vbf)
        from_above = from_behind(down, "sec", -1)
        inner = jnp.einsum("wij,jk->wik", lenv[:WD], vbf, preferred_element_type=f32).astype(bf16)
        diag = jnp.einsum("wik,wkl->il", inner, renv[:WD], preferred_element_type=f32)
        return mask * (diag + raising(from_below) + from_above.astype(f32))

    bnext = from_behind(right_piece[0, 0], "seg", -1)
    scaled = (left_piece[0, 0].astype(f32) * inverse_values[0, 0][None, :]).astype(bf16)
    start = mask * (jnp.dot(scaled, bnext, preferred_element_type=f32) + guess[0, 0].astype(f32))
    norm_start = lax.psum(jnp.sum(start * start), "sec")
    x = start / jnp.sqrt(norm_start)
    g = apply_op(x)
    prec = precond[0, 0].astype(f32)
    lam = jnp.float32(0.0)
    for step in range(ITERS):
        a = lax.psum(jnp.sum(x * g), "sec")
        p = prec * (g - a * x)
        s = lax.psum(jnp.sum(x * p), "sec")
        q = p - s * x
        qq = lax.psum(jnp.sum(q * q), "sec")
        t = q / jnp.sqrt(qq)
        h = apply_op(t)
        b, c = lax.psum((jnp.sum(x * h), jnp.sum(t * h)), "sec")
        lam = 0.5 * (a + c) - jnp.sqrt((0.5 * (a - c)) ** 2 + b * b)
        coeff_x = c - lam
        coeff_t = -b
        nrm = jnp.sqrt(coeff_x * coeff_x + coeff_t * coeff_t)
        x = (coeff_x * x + coeff_t * t) / nrm
        g = (coeff_x * g + coeff_t * h) / nrm
    highest = lax.Precision.HIGHEST
    frob = jnp.sum(x * x)
    polar = x * lax.rsqrt(frob + 1e-06)
    for step in range(NS_STEPS):
        gram = jnp.dot(polar, polar.T, precision=highest, preferred_element_type=f32)
        polar = 1.5 * polar - 0.5 * jnp.dot(
            gram, polar, precision=highest, preferred_element_type=f32
        )
    weight = jnp.dot(polar.T, x, precision=highest, preferred_element_type=f32).astype(bf16)
    handed = from_behind(weight, "seg", 1)
    return (polar[None, None], handed[None, None], jnp.reshape(lam, (1,)))


def solution(mesh):
    placed = (
        P("seg", "sec", None, None, None),
        P("seg", "sec", None, None, None),
        P("seg", "sec", None, None),
        P("seg", "sec", None, None),
        P("seg", "sec", None, None),
        P("seg", "sec", None),
        P("seg", "sec", None, None),
        P("seg", "sec"),
    )
    return jax.shard_map(
        shards,
        mesh=mesh,
        in_specs=placed,
        out_specs=(P("seg", "sec", None, None), P("seg", "sec", None, None), P("seg")),
        check_vma=False,
    )
```

profile of v0, /device:TPU:1, one launch (start us, length us, event | category | flops | bytes accessed | tf_op | source)
XLA Modules:
  0.0 430.0 jit_solution(5454077836777135044)
XLA Ops:
  0.6 8.8 %collective-permute-start = (bf16[256,256]{1,0:T(8,128)(2,1)}, bf16[256,256]{1,0:T(8,128)(2,1)S(1)}, u32[]{:S(2)}, u32[]{:S(2)}) collective-permute-start(bf16[256,256]{1,0:T(8,128)(2,1)} %bitcast.358), channel_id=1, source_target_pairs={{16,0},{32,16},{48,32},{64,48},{80,64},{96,80},{112,96},{128,112},... | collective-permute-start | bytes 393224 | tf_op jit(solution)/shard_map/ppermute | solution.py:14
  12.4 31.9 %psum.77 = f32[]{:T(128)} all-reduce(f32[]{:T(128)} %get-tuple-element.20), channel_id=1, replica_groups=mesh['seg'=32,'sec'=16] {'sec'}, use_global_device_ids=true, to_apply=%region_1.0 | all-reduce | flops 1 | bytes 8 | tf_op jit(solution)/shard_map/psum | solution.py:52
  46.5 3.7 fusion.192
  52.9 3.0 collective-permute-done.2
  55.9 3.8 multiply_reduce_fusion.10
  59.7 29.1 %psum.78 = f32[]{:T(128)} all-reduce(f32[]{:T(128)} %get-tuple-element.22), channel_id=1, replica_groups=mesh['seg'=32,'sec'=16] {'sec'}, use_global_device_ids=true, to_apply=%region_3.0 | all-reduce | flops 1 | bytes 8 | tf_op jit(solution)/shard_map/psum | solution.py:58
  90.1 30.9 %psum.79 = f32[]{:T(128)} all-reduce(f32[]{:T(128)} %multiply_reduce_fusion.9), channel_id=1, replica_groups=mesh['seg'=32,'sec'=16] {'sec'}, use_global_device_ids=true, to_apply=%region_5.0 | all-reduce | flops 1 | bytes 8 | tf_op jit(solution)/shard_map/psum | solution.py:60
  121.0 2.0 multiply_reduce_fusion.8
  123.0 29.3 %psum.80 = f32[]{:T(128)} all-reduce(f32[]{:T(128)} %multiply_reduce_fusion.8), channel_id=1, replica_groups=mesh['seg'=32,'sec'=16] {'sec'}, use_global_device_ids=true, to_apply=%region_7.0 | all-reduce | flops 1 | bytes 8 | tf_op jit(solution)/shard_map/psum | solution.py:62
  154.3 3.2 fusion.185
  157.5 3.7 collective-permute-start.3
  162.5 2.1 fusion.65
  164.6 2.6 collective-permute-done.4
  167.9 4.0 multiply_reduce_fusion.6
  171.9 29.1 %all-reduce.1 = (f32[]{:T(128)}, f32[]{:T(128)}) all-reduce(f32[]{:T(128)} %get-tuple-element.6, f32[]{:T(128)} %get-tuple-element.5), channel_id=1, replica_groups=mesh['seg'=32,'sec'=16] {'sec'}, use_global_device_ids=true, to_apply=%region_9.0 | all-reduce | flops 2 | bytes 16 | tf_op jit(solution)/shard_map/psum | solution.py:65
  207.0 30.6 %psum.83 = f32[]{:T(128)} all-reduce(f32[]{:T(128)} %get-tuple-element.15), channel_id=1, replica_groups=mesh['seg'=32,'sec'=16] {'sec'}, use_global_device_ids=true, to_apply=%region_13.0 | all-reduce | flops 1 | bytes 8 | tf_op jit(solution)/shard_map/psum | solution.py:58
  238.9 29.5 %psum.84 = f32[]{:T(128)} all-reduce(f32[]{:T(128)} %multiply_reduce_fusion.4), channel_id=1, replica_groups=mesh['seg'=32,'sec'=16] {'sec'}, use_global_device_ids=true, to_apply=%region_15.0 | all-reduce | flops 1 | bytes 8 | tf_op jit(solution)/shard_map/psum | solution.py:60
  270.4 30.5 %psum.85 = f32[]{:T(128)} all-reduce(f32[]{:T(128)} %multiply_reduce_fusion.3), channel_id=1, replica_groups=mesh['seg'=32,'sec'=16] {'sec'}, use_global_device_ids=true, to_apply=%region_17.0 | all-reduce | flops 1 | bytes 8 | tf_op jit(solution)/shard_map/psum | solution.py:62
  302.9 3.9 fusion.178
  306.8 2.6 collective-permute-start.5
  312.1 3.0 collective-permute-done.6
  315.1 3.8 multiply_reduce_fusion.1
  318.9 29.4 %all-reduce = (f32[]{:T(128)}, f32[]{:T(128)}) all-reduce(f32[]{:T(128)} %get-tuple-element.4, f32[]{:T(128)} %get-tuple-element.3), channel_id=1, replica_groups=mesh['seg'=32,'sec'=16] {'sec'}, use_global_device_ids=true, to_apply=%region_19.0 | all-reduce | flops 2 | bytes 16 | tf_op jit(solution)/shard_map/psum | solution.py:65
  358.0 68.2 %collective-permute-start.7 = (bf16[256,256]{1,0:T(8,128)(2,1)S(1)}, bf16[256,256]{1,0:T(8,128)(2,1)S(1)}, u32[]{:S(2)}, u32[]{:S(2)}) collective-permute-start(bf16[256,256]{1,0:T(8,128)(2,1)S(1)} %convolution_convert_fusion.3), channel_id=1, source_target_pairs={{0,16},{16,32},{32,48},{48,64},{64,80},{80,96},{96,112},{112,128},... | collective-permute-start | bytes 393224 | tf_op jit(solution)/shard_map/ppermute | solution.py:14
  (39 shorter events, 25.4 us)
Async XLA Ops:
  0.6 10.0 %collective-permute-start = (bf16[256,256]{1,0:T(8,128)(2,1)}, bf16[256,256]{1,0:T(8,128)(2,1)S(1)}, u32[]{:S(2)}, u32[]{:S(2)}) collective-permute-start(bf16[256,256]{1,0:T(8,128)(2,1)} %bitcast.358), channel_id=1, source_target_pairs={{16,0},{32,16},{48,32},{64,48},{80,64},{96,80},{112,96},{128,112},... | collective-permute-start | bytes 393224 | tf_op jit(solution)/shard_map/ppermute | solution.py:14
  45.0 6.5 %copy-start.2 = (bf16[1,1,16,256,256]{4,3,2,1,0:T(8,128)(2,1)S(1)}, bf16[1,1,16,256,256]{4,3,2,1,0:T(8,128)(2,1)}, u32[]{:S(2)}) copy-start(bf16[1,1,16,256,256]{4,3,2,1,0:T(8,128)(2,1)} %param.9) | copy-start | bytes 6291460
  45.0 10.9 %collective-permute-start.1 = (bf16[256,256]{1,0:T(8,128)(2,1)S(1)}, bf16[256,256]{1,0:T(8,128)(2,1)S(1)}, u32[]{:S(2)}, u32[]{:S(2)}) collective-permute-start(bf16[256,256]{1,0:T(8,128)(2,1)S(1)} %fusion.262), channel_id=1, source_target_pairs={{0,1},{1,2},{2,3},{3,4},{4,5},{5,6},{6,7},{7,8},{8,9},{9,10},{10,1... | collective-permute-start | bytes 393224 | tf_op jit(solution)/shard_map/ppermute | solution.py:14
  50.2 5.7 %collective-permute-start.2 = (bf16[256,256]{1,0:T(8,128)(2,1)S(1)}, bf16[256,256]{1,0:T(8,128)(2,1)S(1)}, u32[]{:S(2)}, u32[]{:S(2)}) collective-permute-start(bf16[256,256]{1,0:T(8,128)(2,1)S(1)} %fusion.192), channel_id=1, source_target_pairs={{1,0},{2,1},{3,2},{4,3},{5,4},{6,5},{7,6},{8,7},{9,8},{10,9},{11,1... | collective-permute-start | bytes 393224 | tf_op jit(solution)/shard_map/ppermute | solution.py:14
  52.9 35.9 %copy-start = (bf16[1,1,256,256]{3,2,1,0:T(8,128)(2,1)S(1)}, bf16[1,1,256,256]{3,2,1,0:T(8,128)(2,1)}, u32[]{:S(2)}) copy-start(bf16[1,1,256,256]{3,2,1,0:T(8,128)(2,1)} %param.14) | copy-start | bytes 393220
  157.5 9.8 %collective-permute-start.3 = (bf16[256,256]{1,0:T(8,128)(2,1)S(1)}, bf16[256,256]{1,0:T(8,128)(2,1)S(1)}, u32[]{:S(2)}, u32[]{:S(2)}) collective-permute-start(bf16[256,256]{1,0:T(8,128)(2,1)S(1)} %get-tuple-element.18), channel_id=1, source_target_pairs={{0,1},{1,2},{2,3},{3,4},{4,5},{5,6},{6,7},{7,8},{8,9},{9,10},{10,1... | collective-permute-start | bytes 393224 | tf_op jit(solution)/shard_map/ppermute | solution.py:14
  161.2 6.0 %collective-permute-start.4 = (bf16[256,256]{1,0:T(8,128)(2,1)S(1)}, bf16[256,256]{1,0:T(8,128)(2,1)S(1)}, u32[]{:S(2)}, u32[]{:S(2)}) collective-permute-start(bf16[256,256]{1,0:T(8,128)(2,1)S(1)} %fusion.185), channel_id=1, source_target_pairs={{1,0},{2,1},{3,2},{4,3},{5,4},{6,5},{7,6},{8,7},{9,8},{10,9},{11,1... | collective-permute-start | bytes 393224 | tf_op jit(solution)/shard_map/ppermute | solution.py:14
  167.3 0.7 copy-start.4
  302.9 7.8 %copy-start.3 = (bf16[1,1,16,256,256]{4,3,2,1,0:T(8,128)(2,1)S(1)}, bf16[1,1,16,256,256]{4,3,2,1,0:T(8,128)(2,1)}, u32[]{:S(2)}) copy-start(bf16[1,1,16,256,256]{4,3,2,1,0:T(8,128)(2,1)} %param.9) | copy-start | bytes 6291460
  306.8 8.4 %collective-permute-start.5 = (bf16[256,256]{1,0:T(8,128)(2,1)S(1)}, bf16[256,256]{1,0:T(8,128)(2,1)S(1)}, u32[]{:S(2)}, u32[]{:S(2)}) collective-permute-start(bf16[256,256]{1,0:T(8,128)(2,1)S(1)} %get-tuple-element.13), channel_id=1, source_target_pairs={{0,1},{1,2},{2,3},{3,4},{4,5},{5,6},{6,7},{7,8},{8,9},{9,10},{10,1... | collective-permute-start | bytes 393224 | tf_op jit(solution)/shard_map/ppermute | solution.py:14
  309.4 5.7 %collective-permute-start.6 = (bf16[256,256]{1,0:T(8,128)(2,1)S(1)}, bf16[256,256]{1,0:T(8,128)(2,1)S(1)}, u32[]{:S(2)}, u32[]{:S(2)}) collective-permute-start(bf16[256,256]{1,0:T(8,128)(2,1)S(1)} %fusion.178), channel_id=1, source_target_pairs={{1,0},{2,1},{3,2},{4,3},{5,4},{6,5},{7,6},{8,7},{9,8},{10,9},{11,1... | collective-permute-start | bytes 393224 | tf_op jit(solution)/shard_map/ppermute | solution.py:14
  357.4 71.4 %copy-start.1 = (f32[256,256]{1,0:T(8,128)}, f32[256,256]{1,0:T(8,128)S(1)}, u32[]{:S(2)}) copy-start(f32[256,256]{1,0:T(8,128)S(1)} %fusion.69) | copy-start | bytes 786436
  358.0 70.2 %collective-permute-start.7 = (bf16[256,256]{1,0:T(8,128)(2,1)S(1)}, bf16[256,256]{1,0:T(8,128)(2,1)S(1)}, u32[]{:S(2)}, u32[]{:S(2)}) collective-permute-start(bf16[256,256]{1,0:T(8,128)(2,1)S(1)} %convolution_convert_fusion.3), channel_id=1, source_target_pairs={{0,16},{16,32},{32,48},{48,64},{64,80},{80,96},{96,112},{112,128},... | collective-permute-start | bytes 393224 | tf_op jit(solution)/shard_map/ppermute | solution.py:14
where the time goes:
time: 434 us; the launch traced here: 430 us
  blocking collectives  270 us (62%)
  starting transfers between devices  88.7 us (20%)
  matrix products  32 us (7%)
  between operations  15.9 us (4%)
  waiting for transfers between devices  11.1 us (3%)
  other arithmetic  10.7 us (2%)
    ppermute x8, starting transfers between devices, from_behind(): lax.ppermute(value, axis, [(source, source + steps) for source in range(f...  88.7 us
    psum x2, blocking collectives, shards(): s = lax.psum(jnp.sum(x * p), 'sec')  60.4 us
    psum x2, blocking collectives, shards(): qq = lax.psum(jnp.sum(q * q), 'sec')  59.7 us
    psum x2, blocking collectives, shards(): a = lax.psum(jnp.sum(x * g), 'sec')  59.7 us
    psum x2, blocking collectives, shards(): b, c = lax.psum((jnp.sum(x * h), jnp.sum(t * h)), 'sec')  58.5 us
    psum x1, blocking collectives, shards(): norm_start = lax.psum(jnp.sum(start * start), 'sec')  31.9 us
    dot_general x3, matrix products, raising(): return jnp.einsum('wik,wkl->il', inner, rraise, preferred_element_type=f32)  11.6 us
    ppermute x8, waiting for transfers between devices, from_behind(): lax.ppermute(value, axis, [(source, source + steps) for source in range(f...  11.1 us
  transfers between devices with their start and end apart: 8, of which 5 were waited for; matrix products, arithmetic and copies ran while one was open for 2% of the time, Pallas kernels for 0%

commit v1 on v0

v1 whole, which is shorter than its diff:
```python
import functools

import jax
import jax.numpy as jnp
from jax import lax
from jax.experimental import pallas as pl
from jax.experimental.pallas import tpu as pltpu
from jax.sharding import PartitionSpec as P

WD = 2
ITERS = 2
NS_STEPS = 3
F32 = jnp.float32
BF16 = jnp.bfloat16
SHRINK = 2.0 ** -18
MESH = pl.DeviceIdType.MESH


def nn(a, b):
    return jnp.dot(a, b, preferred_element_type=F32)


def nt(a, b):
    return lax.dot_general(a, b, (((1,), (1,)), ((), ())), preferred_element_type=F32)


def tn(a, b):
    return lax.dot_general(a, b, (((0,), (0,)), ((), ())), preferred_element_type=F32)


def split(a):
    high = a.astype(BF16)
    return high, (a - high.astype(F32)).astype(BF16)


def three(dot, a, b):
    return dot(a[0], b[0]) + (dot(a[0], b[1]) + dot(a[1], b[0]))


def column_sum(value):
    size = value.shape[1]
    row = jnp.sum(value, axis=0, keepdims=True)
    total = row[:, :128]
    for at in range(128, size, 128):
        total = total + row[:, at:at + 128]
    return total


def kernel(
    segs, secs, lenv_hbm, renv_hbm, lpiece, rpiece_hbm, guess, inv, prec, rows,
    polar_out, handed_out, lam_out,
    lenv, renv, inner, bnext, vsend, vrecv, dsend, drecv, part, gathered, wsend,
    r_ref, g_ref, x_ref, t_ref, d_ref, zero_ref,
    load_sem, seg_send, seg_recv, v_send, v_recv, d_send, d_recv, ar_send, ar_recv, out_sem,
):
    seg = lax.axis_index("seg")
    sec = lax.axis_index("sec")
    channels, size = lenv.shape[0], lenv.shape[1]
    half = size // 2

    loads = [
        pltpu.make_async_copy(lenv_hbm.at[0, 0], lenv, load_sem.at[0]),
        pltpu.make_async_copy(renv_hbm.at[0, 0], renv, load_sem.at[1]),
    ]
    for load in loads:
        load.start()

    above = lax.rem(sec + 1, secs)
    below = lax.rem(sec + secs - 1, secs)
    ahead = lax.rem(seg + 1, segs)
    behind = lax.rem(seg + segs - 1, segs)
    barrier = pltpu.get_barrier_semaphore()
    for step in range(1, secs):
        pl.semaphore_signal(
            barrier, inc=1, device_id={"sec": lax.rem(sec + step, secs)}, device_id_type=MESH
        )
    for other in (ahead, behind):
        pl.semaphore_signal(barrier, inc=1, device_id={"seg": other}, device_id_type=MESH)
    pl.semaphore_wait(barrier, secs + 1)

    fetch = pltpu.make_async_remote_copy(
        src_ref=rpiece_hbm.at[0, 0], dst_ref=bnext, send_sem=seg_send.at[0],
        recv_sem=seg_recv.at[0], device_id={"seg": behind}, device_id_type=MESH,
    )
    fetch.start()

    count = rows[0, 0]
    idx_r = lax.broadcasted_iota(jnp.int32, (size, size), 0)
    idx_c = lax.broadcasted_iota(jnp.int32, (size, size), 1)
    alive = (idx_r < count) & (idx_c < count)
    has_below = sec > 0
    has_above = sec < secs - 1

    def up_copy(k, src, dst):
        return pltpu.make_async_remote_copy(
            src_ref=src, dst_ref=dst, send_sem=v_send.at[k], recv_sem=v_recv.at[k],
            device_id={"sec": above}, device_id_type=MESH,
        )

    def down_copy(k, src, dst):
        return pltpu.make_async_remote_copy(
            src_ref=src, dst_ref=dst, send_sem=d_send.at[k], recv_sem=d_recv.at[k],
            device_id={"sec": below}, device_id_type=MESH,
        )

    def inner_of(value, first, last):
        width = value.shape[1]
        for w in range(first, last):
            inner[:, w * size:w * size + width] = nn(lenv[w], value).astype(BF16)

    def outer_of(first, last):
        total = None
        for w in range(first, last):
            term = nn(inner[:, w * size:(w + 1) * size], renv[w])
            total = term if total is None else total + term
        return total

    def apply_op(k):
        vec = vsend[k]
        inner_of(vec, 0, channels)
        dsend[k] = outer_of(WD, channels).astype(BF16)
        down = down_copy(k, dsend.at[k], drecv.at[k])
        down.start()
        diag = outer_of(0, WD)
        return diag, down

    def finish_op(k, up, down, diag):
        up.wait_recv()
        inner_of(vrecv[k], WD, channels)
        raised = outer_of(WD, channels)
        down.wait_recv()
        lowered = drecv[k].astype(F32)
        return diag + jnp.where(has_below, raised, 0.0) + jnp.where(has_above, lowered, 0.0)

    def put(k, row, value):
        part[k, row:row + 1, :] = column_sum(value)

    def exchange(k):
        gathered[k, sec] = part[k]
        copies = []
        for step in range(1, secs):
            copy = pltpu.make_async_remote_copy(
                src_ref=part.at[k], dst_ref=gathered.at[k, sec],
                send_sem=ar_send.at[k, step], recv_sem=ar_recv.at[k, step],
                device_id={"sec": lax.rem(sec + step, secs)}, device_id_type=MESH,
            )
            copy.start()
            copies.append(copy)
        return copies

    def totals(k, copies):
        for copy in copies:
            copy.wait_recv()
        return jnp.sum(jnp.sum(gathered[k], axis=0), axis=1, keepdims=True)

    part[...] = jnp.zeros_like(part)
    d = prec[0, 0].astype(F32)
    d_ref[...] = d
    scaled = (lpiece[0, 0].astype(F32) * inv[0]).astype(BF16)
    fetch.wait_recv()
    joined = jnp.where(seg < segs - 1, nn(scaled, bnext[...]), 0.0)
    r = jnp.where(alive, joined + guess[0, 0].astype(F32), 0.0)
    r_ref[...] = r
    vsend[0] = r.astype(BF16)
    up0 = up_copy(0, vsend.at[0], vrecv.at[0])
    up0.start()
    for load in loads:
        load.wait()
    diag, down0 = apply_op(0)
    dr = d * r
    put(0, 0, r * r)
    put(0, 1, dr * r)
    put(0, 2, dr * dr)
    big_g = jnp.where(alive, SHRINK * finish_op(0, up0, down0, diag), 0.0)
    r = r_ref[...]
    d = d_ref[...]
    dr = d * r
    dg = d * big_g
    put(0, 3, r * big_g)
    put(0, 4, dr * big_g)
    put(0, 5, dg * dg)
    put(0, 6, dg * dr)
    g_ref[...] = big_g
    ex0 = exchange(0)
    tot = totals(0, ex0)
    n0 = tot[0:1]
    grow = 1.0 / SHRINK
    scale = 1.0 / jnp.sqrt(n0)
    over = 1.0 / n0
    over_g = grow * over
    x_dx = tot[1:2] * over
    dx_dx = tot[2:3] * over
    a = tot[3:4] * over_g
    x_dg = tot[4:5] * over_g
    dg_dg = tot[5:6] * over_g * grow
    dg_dx = tot[6:7] * over_g

    def correction(a, x_dx, x_dg, dx_dx, dg_dx, dg_dg):
        s = x_dg - a * x_dx
        pp = dg_dg - 2.0 * a * dg_dx + a * a * dx_dx
        qq = jnp.maximum(pp - s * s, 1e-7 * (dg_dg + a * a * dx_dx))
        return s, 1.0 / jnp.sqrt(qq)

    s, over_q = correction(a, x_dx, x_dg, dx_dx, dg_dx, dg_dg)
    x = r_ref[...] * scale
    g = g_ref[...] * (scale * grow)
    d = d_ref[...]
    t = (d * (g - a * x) - s * x) * over_q
    vsend[1] = t.astype(BF16)
    up1 = up_copy(1, vsend.at[1], vrecv.at[1])
    up1.start()
    x_ref[...] = x
    g_ref[...] = g
    t_ref[...] = t
    diag, down1 = apply_op(1)
    d = d_ref[...]
    x = x_ref[...]
    g = g_ref[...]
    t = t_ref[...]
    dt = d * t
    put(1, 0, t * t)
    put(1, 1, dt * t)
    put(1, 2, dt * x)
    put(1, 3, dt * g)
    put(1, 4, dt * dt)
    put(1, 5, dt * (d * x))
    put(1, 6, dt * (d * g))
    put(1, 7, t * g)
    h = jnp.where(alive, finish_op(1, up1, down1, diag), 0.0)
    d = d_ref[...]
    x = x_ref[...]
    g = g_ref[...]
    t = t_ref[...]
    dh = d * h
    put(1, 8, t * h)
    put(1, 9, x * h)
    put(1, 10, x * dh)
    put(1, 11, t * dh)
    put(1, 12, dh * dh)
    put(1, 13, dh * (d * g))
    put(1, 14, dh * (d * x))
    put(1, 15, dh * (d * t))
    r_ref[...] = h
    ex1 = exchange(1)
    tot = totals(1, ex1)

    def ritz(a, b, c):
        lam = 0.5 * (a + c) - jnp.sqrt((0.5 * (a - c)) ** 2 + b * b)
        u = c - lam
        w = -b
        over = 1.0 / jnp.sqrt(u * u + w * w)
        return lam, u * over, w * over

    tau = 1.0 / jnp.sqrt(tot[0:1])
    lam, al, be = ritz(a, tot[9:10] * tau, tot[8:9] * tau * tau)
    be = be * tau
    aa, ab, bb = al * al, al * be, be * be
    a = aa * a + ab * (tot[9:10] + tot[7:8]) + bb * tot[8:9]
    x_dx = aa * x_dx + 2.0 * ab * tot[2:3] + bb * tot[1:2]
    x_dg = aa * x_dg + ab * (tot[10:11] + tot[3:4]) + bb * tot[11:12]
    dg_dg = aa * dg_dg + 2.0 * ab * tot[13:14] + bb * tot[12:13]
    dg_dx = aa * dg_dx + ab * (tot[6:7] + tot[14:15]) + bb * tot[15:16]
    dx_dx = aa * dx_dx + 2.0 * ab * tot[5:6] + bb * tot[4:5]
    s, over_q = correction(a, x_dx, x_dg, dx_dx, dg_dx, dg_dg)
    x = al * x_ref[...] + be * t_ref[...]
    g = al * g_ref[...] + be * r_ref[...]
    t = (d_ref[...] * (g - a * x) - s * x) * over_q
    vsend[2] = t.astype(BF16)
    up2 = up_copy(2, vsend.at[2, :, :half], vrecv.at[2, :, :half])
    up2.start()
    x_ref[...] = x
    t_ref[...] = t
    put(2, 0, t * t)
    put(2, 1, t * g)
    inner_of(vsend[2], 0, channels)
    lower = None
    for w in range(WD, channels):
        term = nn(inner[:, w * size:(w + 1) * size], renv[w, :, half:])
        lower = term if lower is None else lower + term
    dsend[2, :, half:] = lower.astype(BF16)
    down2 = down_copy(2, dsend.at[2, :, half:], drecv.at[2, :, half:])
    down2.start()
    diag = outer_of(0, WD)
    up2.wait_recv()
    inner_of(vrecv[2, :, :half], WD, channels)
    upper = None
    for w in range(WD, channels):
        term = nn(inner[:, w * size:w * size + half], renv[w, :half, :])
        upper = term if upper is None else upper + term
    t = t_ref[...]
    put(2, 2, t * (diag + 2.0 * jnp.where(has_below, upper, 0.0)))
    down2.wait_recv()
    put(2, 3, jnp.concatenate([
        2.0 * t[:, half:] * jnp.where(has_above, drecv[2, :, half:].astype(F32), 0.0)
    ], axis=1))
    ex2 = exchange(2)
    tot = totals(2, ex2)
    tau = 1.0 / jnp.sqrt(tot[0:1])
    lam, al, be = ritz(a, tot[1:2] * tau, (tot[2:3] + tot[3:4]) * tau * tau)
    be = be * tau
    lam_out[0] = lam[0, 0]
    x = al * x_ref[...] + be * t_ref[...]
    x_ref[...] = x
    frob = jnp.sum(jnp.sum(x * x, axis=0, keepdims=True), axis=1, keepdims=True)
    polar = x * lax.rsqrt(frob + 1e-06)
    for step in range(NS_STEPS):
        pair = split(polar)
        gram = three(nt, pair, pair)
        polar = 1.5 * polar - 0.5 * three(nn, split(gram), pair)
    r_ref[...] = polar
    polar_copy = pltpu.make_async_copy(r_ref, polar_out.at[0, 0], out_sem.at[0])
    polar_copy.start()
    weight = three(tn, split(polar), split(x_ref[...]))
    wsend[...] = weight.astype(BF16)
    hand = pltpu.make_async_remote_copy(
        src_ref=wsend, dst_ref=handed_out.at[0, 0], send_sem=seg_send.at[1],
        recv_sem=seg_recv.at[1], device_id={"seg": ahead}, device_id_type=MESH,
    )

    @pl.when(seg < segs - 1)
    def _():
        hand.start()

    @pl.when(seg == 0)
    def _():
        zero_ref[...] = jnp.zeros_like(zero_ref)
        clear = pltpu.make_async_copy(zero_ref, handed_out.at[0, 0], out_sem.at[1])
        clear.start()
        clear.wait()

    fetch.wait_send()
    for copy in (up0, down0, up1, down1, up2, down2):
        copy.wait_send()
    for copy in ex0 + ex1 + ex2:
        copy.wait_send()
    polar_copy.wait()

    @pl.when(seg < segs - 1)
    def _():
        hand.wait_send()

    @pl.when(seg > 0)
    def _():
        hand.wait_recv()


def shards(segs, secs, left_env, right_env, left_piece, right_piece, guess, inverse_values,
           precond, sector_rows):
    channels, size = left_env.shape[2], left_env.shape[3]
    vmem = pl.BlockSpec(memory_space=pltpu.VMEM)
    smem = pl.BlockSpec(memory_space=pltpu.SMEM)
    hbm = pl.BlockSpec(memory_space=pl.ANY)
    square = (size, size)
    return pl.pallas_call(
        functools.partial(kernel, segs, secs),
        out_shape=(
            jax.ShapeDtypeStruct((1, 1) + square, F32),
            jax.ShapeDtypeStruct((1, 1) + square, BF16),
            jax.ShapeDtypeStruct((1,), F32),
        ),
        in_specs=[hbm, hbm, vmem, hbm, vmem, vmem, vmem, smem],
        out_specs=(hbm, hbm, smem),
        scratch_shapes=[
            pltpu.VMEM((channels,) + square, BF16),
            pltpu.VMEM((channels,) + square, BF16),
            pltpu.VMEM((size, channels * size), BF16),
            pltpu.VMEM(square, BF16),
            pltpu.VMEM((3,) + square, BF16),
            pltpu.VMEM((3,) + square, BF16),
            pltpu.VMEM((3,) + square, BF16),
            pltpu.VMEM((3,) + square, BF16),
            pltpu.VMEM((3, 16, 128), F32),
            pltpu.VMEM((3, secs, 16, 128), F32),
            pltpu.VMEM(square, BF16),
            pltpu.VMEM(square, F32),
            pltpu.VMEM(square, F32),
            pltpu.VMEM(square, F32),
            pltpu.VMEM(square, F32),
            pltpu.VMEM(square, F32),
            pltpu.VMEM(square, BF16),
            pltpu.SemaphoreType.DMA((2,)),
            pltpu.SemaphoreType.DMA((2,)),
            pltpu.SemaphoreType.DMA((2,)),
            pltpu.SemaphoreType.DMA((3,)),
            pltpu.SemaphoreType.DMA((3,)),
            pltpu.SemaphoreType.DMA((3,)),
            pltpu.SemaphoreType.DMA((3,)),
            pltpu.SemaphoreType.DMA((3, secs)),
            pltpu.SemaphoreType.DMA((3, secs)),
            pltpu.SemaphoreType.DMA((2,)),
        ],
        compiler_params=pltpu.CompilerParams(
            collective_id=0, has_side_effects=True, vmem_limit_bytes=60 * 1024 * 1024
        ),
        cost_estimate=pl.CostEstimate(
            flops=3 * 60 * 2 * size ** 3, bytes_accessed=6 * 1024 * 1024, transcendentals=0
        ),
    )(left_env, right_env, left_piece, right_piece, guess, inverse_values, precond, sector_rows)


def solution(mesh):
    placed = (
        P("seg", "sec", None, None, None),
        P("seg", "sec", None, None, None),
        P("seg", "sec", None, None),
        P("seg", "sec", None, None),
        P("seg", "sec", None, None),
        P("seg", "sec", None),
        P("seg", "sec", None, None),
        P("seg", "sec"),
    )
    return jax.shard_map(
        functools.partial(shards, mesh.shape["seg"], mesh.shape["sec"]),
        mesh=mesh,
        in_specs=placed,
        out_specs=(P("seg", "sec", None, None), P("seg", "sec", None, None), P("seg")),
        check_vma=False,
    )
```

time: 434 us -> 62.1 us (0.14)
  blocking collectives: 270 us -> 0 us
  starting transfers between devices: 88.7 us -> 0 us
  Pallas kernels: 0 us -> 55.6 us
  matrix products: 32 us -> 0 us
  between operations: 15.9 us -> 3.04 us
  waiting for transfers between devices: 11.1 us -> 0 us
  other arithmetic: 10.7 us -> 0 us
    psum x9 -> x0, blocking collectives: 270 us -> none  [the longest x2 60.4 us: shards(): s = lax.psum(jnp.sum(x * p), 'sec')]
    ppermute x8 -> x0, starting transfers between devices: 88.7 us -> none  [from_behind(): lax.ppermute(value, axis, [(source, source + steps) for source in range(f...]
    pallas_call x0 -> x1, Pallas kernels: none -> 55.6 us  [shards(): pl.pallas_call(functools.partial(kernel, segs, secs), out_shape=(jax.Shap...]
    dot_general x17 -> x0, matrix products: 32 us -> none  [the longest x3 11.6 us: raising(): return jnp.einsum('wik,wkl->il', inner, rraise, preferred_element_type=f32)]
    ppermute x8 -> x0, waiting for transfers between devices: 11.1 us -> none  [from_behind(): lax.ppermute(value, axis, [(source, source + steps) for source in range(f...]
    reduce_sum x6 -> x0, other arithmetic: 7.94 us -> none  [the longest x2 3.93 us: shards(): qq = lax.psum(jnp.sum(q * q), 'sec')]
  transfers between devices with their start and end apart: 8 -> 0, of which waited for: 5 -> 0; matrix products, arithmetic and copies ran while one was open for 2% -> 0% of each run, Pallas kernels for 0% -> 0%
where the time goes in v1:
time: 62.1 us; the launch traced here: 61.9 us
  Pallas kernels  55.6 us (90%)
  local copies, waits for them, and re-layouts  3.24 us (5%)
  between operations  3.04 us (5%)
    pallas_call x1, Pallas kernels, shards(): pl.pallas_call(functools.partial(kernel, segs, secs), out_shape=(jax.Shap...  55.6 us
    unnamed x2, local copies, waits for them, and re-layouts  3.24 us

profile of v1, /device:TPU:1, one launch (start us, length us, event | category | flops | bytes accessed | tf_op | source)
XLA Modules:
  0.0 61.9 jit_solution(13409397681599052913)
XLA Ops:
  1.3 55.6 %shard_map.103 = (f32[1,1,256,256]{3,2,1,0:T(8,128)}, bf16[1,1,256,256]{3,2,1,0:T(8,128)(2,1)}, f32[1]{0:T(128)}) custom-call(bf16[1,1,16,256,256]{4,3,2,1,0:T(8,128)(2,1)} %lenv_hbm.1, bf16[1,1,16,256,256]{4,3,2,1,0:T(8,128)(2,1)} %renv_hbm.1, bf16[1,1,256,256]{3,2,1,0:T(8,128)(2,1)} %lpiece.1, bf16[1,1,256,256]{3,2,1,0:T(8,128)(2,1)} %rpiece_hbm.1, ...), custom_call_target="tpu_custom_call" | custom-call | flops 6039797760 | bytes 6291456 | tf_op jit(solution)/shard_map/pallas_call | solution.py:354
  56.9 1.7 %copy.15 = f32[1,1,256,256]{3,2,1,0:T(8,128)} copy(f32[1,1,256,256]{3,2,1,0:T(8,128)} %get-tuple-element.6) | data formatting | bytes 524288
  58.5 1.6 %copy.16 = bf16[1,1,256,256]{3,2,1,0:T(8,128)(2,1)} copy(bf16[1,1,256,256]{3,2,1,0:T(8,128)(2,1)} %get-tuple-element.7) | data formatting | bytes 262144

commit v2 on v1

v2 whole, which is shorter than its diff:
```python
import functools

import jax
import jax.numpy as jnp
from jax import lax
from jax.experimental import pallas as pl
from jax.experimental.pallas import tpu as pltpu
from jax.sharding import PartitionSpec as P

WD = 2
ITERS = 2
NS_STEPS = 3
F32 = jnp.float32
BF16 = jnp.bfloat16
SHRINK = 2.0 ** -18
MESH = pl.DeviceIdType.MESH


def nn(a, b):
    return jnp.dot(a, b, preferred_element_type=F32)


def nt(a, b):
    return lax.dot_general(a, b, (((1,), (1,)), ((), ())), preferred_element_type=F32)


def tn(a, b):
    return lax.dot_general(a, b, (((0,), (0,)), ((), ())), preferred_element_type=F32)


def split(a):
    high = a.astype(BF16)
    return high, (a - high.astype(F32)).astype(BF16)


def three(dot, a, b):
    return dot(a[0], b[0]) + (dot(a[0], b[1]) + dot(a[1], b[0]))


def column_sum(value):
    size = value.shape[1]
    row = jnp.sum(value, axis=0, keepdims=True)
    total = row[:, :128]
    for at in range(128, size, 128):
        total = total + row[:, at:at + 128]
    return total


def kernel(
    segs, secs, lenv_hbm, renv_hbm, lpiece_hbm, rpiece_hbm, guess_hbm, inv_hbm, prec_hbm, rows_hbm,
    polar_out, handed_out, lam_out,
    lenv, renv, lpiece, guess, inv, prec, rows, inner_a, inner_b, inner_c, bnext, d_below,
    vsend, vrecv, dsend, drecv, part, gathered, wsend,
    r_ref, g_ref, e_ref, x_ref, t_ref, h_ref, d_ref, k0_ref, k1_ref, hdg_ref, dh_ref, dt_ref, zero_ref, lam_ref,
    load_sem, seg_send, seg_recv, v_send, v_recv, d_send, d_recv, ar_send, ar_recv, out_sem,
):
    seg = lax.axis_index("seg")
    sec = lax.axis_index("sec")
    channels, size = lenv.shape[0], lenv.shape[1]
    half = size // 2

    moves = (
        (rows_hbm, rows), (prec_hbm.at[0, 0], prec), (lpiece_hbm.at[0, 0], lpiece),
        (inv_hbm.at[0], inv), (guess_hbm.at[0, 0], guess), (lenv_hbm.at[0, 0], lenv),
        (renv_hbm.at[0, 0], renv),
    )
    loads = [
        pltpu.make_async_copy(src, dst, load_sem.at[at]) for at, (src, dst) in enumerate(moves)
    ]
    for load in loads:
        load.start()

    above = lax.rem(sec + 1, secs)
    below = lax.rem(sec + secs - 1, secs)
    ahead = lax.rem(seg + 1, segs)
    behind = lax.rem(seg + segs - 1, segs)
    barrier = pltpu.get_barrier_semaphore()
    for step in range(1, secs):
        pl.semaphore_signal(
            barrier, inc=1, device_id={"sec": lax.rem(sec + step, secs)}, device_id_type=MESH
        )
    for other in (ahead, behind):
        pl.semaphore_signal(barrier, inc=1, device_id={"seg": other}, device_id_type=MESH)
    part[...] = jnp.zeros_like(part)
    for load in loads[:5]:
        load.wait()
    d_ref[...] = prec[...].astype(F32)
    scaled = (lpiece[...].astype(F32) * inv[...]).astype(BF16)
    pl.semaphore_wait(barrier, secs + 1)

    fetch = pltpu.make_async_remote_copy(
        src_ref=rpiece_hbm.at[0, 0], dst_ref=bnext, send_sem=seg_send.at[0],
        recv_sem=seg_recv.at[0], device_id={"seg": behind}, device_id_type=MESH,
    )
    fetch.start()

    count = rows[0, 0]
    idx_r = lax.broadcasted_iota(jnp.int32, (size, size), 0)
    idx_c = lax.broadcasted_iota(jnp.int32, (size, size), 1)
    alive = (idx_r < count) & (idx_c < count)
    has_below = sec > 0
    has_above = sec < secs - 1
    top, bottom = slice(0, half), slice(half, size)
    sent = []

    def send(src, dst, target, send_sem, recv_sem):
        copy = pltpu.make_async_remote_copy(
            src_ref=src, dst_ref=dst, send_sem=send_sem, recv_sem=recv_sem,
            device_id=target, device_id_type=MESH,
        )
        copy.start()
        sent.append(copy)
        return copy

    def send_up(k, part_of, value):
        vsend[k, part_of] = value.astype(BF16)
        at = 2 * k + (part_of.start > 0)
        return send(
            vsend.at[k, part_of], vrecv.at[k, part_of], {"sec": above}, v_send.at[at], v_recv.at[at]
        )

    def send_down(k, part_of):
        at = 2 * k + (part_of.start > 0)
        return send(
            dsend.at[k, part_of], drecv.at[k, part_of], {"sec": below}, d_send.at[at], d_recv.at[at]
        )

    def span(first, last):
        return slice(first * size, last * size)

    def lower(k, value, part_of):
        for w in range(WD, channels):
            inner_a[part_of, span(w, w + 1)] = nn(lenv[w, part_of, :], value).astype(BF16)
        flat = renv[WD:].reshape((channels - WD) * size, size)
        dsend[k, part_of] = nn(inner_a[part_of, span(WD, channels)], flat).astype(BF16)

    def diagonal(value):
        for w in range(WD):
            inner_c[:, span(w, w + 1)] = nn(lenv[w], value).astype(BF16)
        return nn(inner_c[...], renv[:WD].reshape(WD * size, size))

    def upper(value):
        for w in range(WD, channels):
            inner_b[:, span(w, w + 1)] = nn(lenv[w], value).astype(BF16)
        return nn(inner_b[:, span(WD, channels)], renv[WD:].reshape((channels - WD) * size, size))

    def upper_part(value, part_of):
        total = None
        for w in range(WD, channels):
            moved = nn(value, renv[w]).astype(BF16)
            term = nn(lenv[w, :, part_of], moved)
            total = term if total is None else total + term
        return total

    def put(k, row, value):
        part[k, row:row + 1, :] = column_sum(value)

    def exchange(k, rows_of):
        gathered[k, sec] = part[k]
        return [
            send(
                part.at[k, :rows_of], gathered.at[k, sec, :rows_of],
                {"sec": lax.rem(sec + step, secs)}, ar_send.at[k, step], ar_recv.at[k, step],
            )
            for step in range(1, secs)
        ]

    def totals(k, copies, rows_of):
        for copy in copies:
            copy.wait_recv()
        return jnp.sum(jnp.sum(gathered[k, :, :rows_of], axis=0), axis=1, keepdims=True)

    def together(diag, raised, k):
        lowered = drecv[k].astype(F32)
        return jnp.where(
            alive,
            diag + jnp.where(has_below, raised, 0.0) + jnp.where(has_above, lowered, 0.0),
            0.0,
        )

    def raised_from(k, copies):
        copies[0].wait_recv()
        total = upper_part(vrecv[k, top], top)
        copies[1].wait_recv()
        return total + upper_part(vrecv[k, bottom], bottom)

    d_copy = send(prec, d_below, {"sec": above}, v_send.at[10], v_recv.at[10])
    fetch.wait_recv()
    up_r = []
    for part_of in (top, bottom):
        joined = jnp.where(seg < segs - 1, nn(scaled[part_of], bnext[...]), 0.0)
        value = jnp.where(alive[part_of], joined + guess[part_of].astype(F32), 0.0)
        r_ref[part_of] = value
        up_r.append(send_up(0, part_of, value))
    for load in loads[5:]:
        load.wait()
    lower(0, vsend[0], top)
    down_r = [send_down(0, top)]
    lower(0, vsend[0], bottom)
    down_r.append(send_down(0, bottom))
    h_ref[...] = diagonal(vsend[0])
    r = r_ref[...]
    e = d_ref[...] * r
    e_ref[...] = e
    vsend[1] = e.astype(BF16)
    put(0, 0, r * r)
    put(0, 1, e * r)
    put(0, 2, e * e)
    lower(1, vsend[1], top)
    lower(1, vsend[1], bottom)
    k0_ref[...] = diagonal(vsend[1])
    raised = raised_from(0, up_r)
    down_e = [send_down(1, top), send_down(1, bottom)]
    for copy in down_r:
        copy.wait_recv()
    big_g = SHRINK * together(h_ref[...], raised, 0)
    g_ref[...] = big_g
    dg = d_ref[...] * big_g
    dh_ref[...] = dg
    up_g = [send_up(2, top, dg[top]), send_up(2, bottom, dg[bottom])]
    put(0, 3, r_ref[...] * big_g)
    put(0, 4, e_ref[...] * big_g)
    put(0, 5, dg * dg)
    put(0, 6, dg * e_ref[...])
    ex0 = exchange(0, 8)
    lower(2, vsend[2], top)
    down_g = [send_down(2, top)]
    lower(2, vsend[2], bottom)
    down_g.append(send_down(2, bottom))
    k1_ref[...] = diagonal(vsend[2])
    d_copy.wait_recv()
    raised = upper((d_below[...].astype(F32) * vrecv[0].astype(F32)).astype(BF16))
    for copy in down_e:
        copy.wait_recv()
    k0_ref[...] = together(k0_ref[...], raised, 1)

    tot = totals(0, ex0, 8)
    n0 = tot[0:1]
    grow = 1.0 / SHRINK
    scale = 1.0 / jnp.sqrt(n0)
    scale_g = scale * grow
    over = 1.0 / n0
    over_g = grow * over
    x_dx = tot[1:2] * over
    dx_dx = tot[2:3] * over
    a = tot[3:4] * over_g
    x_dg = tot[4:5] * over_g
    dg_dg = tot[5:6] * over_g * grow
    dg_dx = tot[6:7] * over_g

    def correction(a, x_dx, x_dg, dx_dx, dg_dx, dg_dg):
        s = x_dg - a * x_dx
        pp = dg_dg - 2.0 * a * dg_dx + a * a * dx_dx
        qq = jnp.maximum(pp - s * s, 1e-7 * (dg_dg + a * a * dx_dx))
        return s, 1.0 / jnp.sqrt(qq)

    s, over_q = correction(a, x_dx, x_dg, dx_dx, dg_dx, dg_dg)
    s_old, q_old, a_old = s, over_q, a
    x = r_ref[...] * scale
    g = g_ref[...] * scale_g
    d = d_ref[...]
    t = (d * (g - a * x) - s * x) * over_q
    x_ref[...] = x
    g_ref[...] = g
    t_ref[...] = t
    dt = d * t
    dt_ref[...] = dt
    vsend[3] = dt.astype(BF16)
    put(1, 0, t * t)
    put(1, 1, dt * t)
    put(1, 2, dt * x)
    put(1, 3, dt * g)
    put(1, 4, dt * dt)
    put(1, 5, dt * (d * x))
    put(1, 6, dt * (d * g))
    put(1, 7, t * g)
    raised = raised_from(2, up_g)
    for copy in down_g:
        copy.wait_recv()
    hdg = together(k1_ref[...], raised, 2) * scale_g
    hdx = k0_ref[...] * scale
    hdg_ref[...] = hdg
    k0_ref[...] = hdx
    g = g_ref[...]
    h = (hdg - a * hdx - s * g) * over_q
    dh = d_ref[...] * h
    vsend[4] = dh.astype(BF16)
    up_h = send_up(4, top, dh[top])
    h_ref[...] = h
    dh_ref[...] = dh
    d = d_ref[...]
    x = x_ref[...]
    t = t_ref[...]
    put(1, 8, t * h)
    put(1, 9, x * h)
    put(1, 10, x * dh)
    put(1, 11, t * dh)
    put(1, 12, dh * dh)
    put(1, 13, dh * (d * g))
    put(1, 14, dh * (d * x))
    put(1, 15, dh * (d * t))
    ex1 = exchange(1, 16)
    lower(4, vsend[4], bottom)
    down_h = send_down(4, bottom)
    lower(3, vsend[3], bottom)
    down_t = send_down(3, bottom)
    k1_ref[...] = diagonal(vsend[4])
    r_ref[...] = diagonal(vsend[3])
    below_d = d_below[top].astype(F32)
    below_x = vrecv[0, top].astype(F32) * scale
    below_g = vrecv[2, top].astype(F32) * scale_g
    below_dt = below_d * ((below_g - (a_old * below_d + s_old) * below_x) * q_old)

    tot = totals(1, ex1, 16)

    def ritz(a, b, c):
        lam = 0.5 * (a + c) - jnp.sqrt((0.5 * (a - c)) ** 2 + b * b)
        u = c - lam
        w = -b
        over = 1.0 / jnp.sqrt(u * u + w * w)
        return lam, u * over, w * over

    tau = 1.0 / jnp.sqrt(tot[0:1])
    lam, al, be = ritz(a, tot[9:10] * tau, tot[8:9] * tau * tau)
    be = be * tau
    aa, ab, bb = al * al, al * be, be * be
    a_old = a
    a = aa * a + ab * (tot[9:10] + tot[7:8]) + bb * tot[8:9]
    x_dx = aa * x_dx + 2.0 * ab * tot[2:3] + bb * tot[1:2]
    x_dg = aa * x_dg + ab * (tot[10:11] + tot[3:4]) + bb * tot[11:12]
    dg_dg = aa * dg_dg + 2.0 * ab * tot[13:14] + bb * tot[12:13]
    dg_dx = aa * dg_dx + ab * (tot[6:7] + tot[14:15]) + bb * tot[15:16]
    dx_dx = aa * dx_dx + 2.0 * ab * tot[5:6] + bb * tot[4:5]
    s, over_q = correction(a, x_dx, x_dg, dx_dx, dg_dx, dg_dg)
    up_h.wait_recv()
    fresh_below = (vrecv[4, top].astype(F32) - a * below_dt).astype(BF16)
    raised = jnp.where(has_below, upper_part(fresh_below, top), 0.0)
    x = al * x_ref[...] + be * t_ref[...]
    g = al * g_ref[...] + be * h_ref[...]
    fresh = be * (dh_ref[...] - a * dt_ref[...])
    known = al * (d_ref[...] * (g_ref[...] - a * x_ref[...])) - s * x
    h_known = al * (hdg_ref[...] - a * k0_ref[...]) - s * g
    t = (known + fresh) * over_q
    put(2, 0, t * t)
    put(2, 1, t * g)
    x_ref[...] = x
    t_ref[...] = t
    diag = be * (k1_ref[...] - a * r_ref[...] + 2.0 * raised)
    put(2, 2, (known + 2.0 * fresh) * h_known + fresh * diag)
    down_t.wait_recv()
    down_h.wait_recv()
    lowered = drecv[4, bottom].astype(F32) - a * drecv[3, bottom].astype(F32)
    put(2, 3, fresh[bottom] * ((2.0 * be) * jnp.where(has_above, lowered, 0.0)))
    ex2 = exchange(2, 8)
    pair_x = split(x_ref[...])
    pair_t = split(t_ref[...])
    k0_ref[...] = three(nt, pair_x, pair_x)
    k1_ref[...] = three(nt, pair_x, pair_t) + three(nt, pair_t, pair_x)
    e_ref[...] = three(nt, pair_t, pair_t)
    g_ref[...] = x_ref[...].T
    h_ref[...] = t_ref[...].T
    def block_sum(value):
        return jnp.sum(jnp.sum(value, axis=0, keepdims=True), axis=1, keepdims=True)

    frob_x = block_sum(x_ref[...] * x_ref[...])
    frob_t = block_sum(t_ref[...] * t_ref[...])
    frob_xt = block_sum(x_ref[...] * t_ref[...])
    tot = totals(2, ex2, 8)
    tau = 1.0 / jnp.sqrt(tot[0:1])
    lam, al, be = ritz(a, tot[1:2] * tau, (tot[2:3] + tot[3:4]) * (over_q * tau) ** 2)
    be = be * tau
    lam_ref[0] = lam[0, 0]
    lam_copy = pltpu.make_async_copy(lam_ref, lam_out, out_sem.at[2])
    lam_copy.start()
    aa, ab, bb = al * al, al * be, be * be
    over = lax.rsqrt(aa * frob_x + 2.0 * ab * frob_xt + bb * frob_t + 1e-06)
    polar = (al * x_ref[...] + be * t_ref[...]) * over
    turned = split(al * g_ref[...] + be * h_ref[...])
    gram = (aa * k0_ref[...] + ab * k1_ref[...] + bb * e_ref[...]) * (over * over)
    for step in range(NS_STEPS):
        pair = split(polar)
        if step:
            gram = three(nt, pair, pair)
        polar = 1.5 * polar - 0.5 * three(nn, split(gram), pair)
    r_ref[...] = polar
    polar_copy = pltpu.make_async_copy(r_ref, polar_out.at[0, 0], out_sem.at[0])
    polar_copy.start()
    pair = split(polar)
    hands = []
    for at, part_of in enumerate((top, bottom)):
        weight = three(nn, (turned[0][part_of], turned[1][part_of]), pair)
        wsend[part_of] = weight.astype(BF16)
        hand = pltpu.make_async_remote_copy(
            src_ref=wsend.at[part_of], dst_ref=handed_out.at[0, 0, part_of],
            send_sem=seg_send.at[1 + at], recv_sem=seg_recv.at[1 + at],
            device_id={"seg": ahead}, device_id_type=MESH,
        )
        hands.append(hand)

        @pl.when(seg < segs - 1)
        def _():
            hand.start()

    @pl.when(seg == 0)
    def _():
        zero_ref[...] = jnp.zeros_like(zero_ref)
        clear = pltpu.make_async_copy(zero_ref, handed_out.at[0, 0], out_sem.at[1])
        clear.start()
        clear.wait()

    fetch.wait_send()
    for copy in sent:
        copy.wait_send()
    polar_copy.wait()
    lam_copy.wait()

    @pl.when(seg < segs - 1)
    def _():
        for hand in hands:
            hand.wait_send()

    @pl.when(seg > 0)
    def _():
        for hand in hands:
            hand.wait_recv()


def store(polar_in, handed_in, lam_in, polar_out, handed_out, lam_out):
    polar_out[...] = polar_in[...]
    handed_out[...] = handed_in[...]
    lam_out[0] = lam_in[0]


def shards(segs, secs, left_env, right_env, left_piece, right_piece, guess, inverse_values,
           precond, sector_rows):
    channels, size = left_env.shape[2], left_env.shape[3]
    hbm = pl.BlockSpec(memory_space=pl.ANY)
    square = (size, size)
    envs = pltpu.VMEM((channels,) + square, BF16)
    block = pltpu.VMEM(square, BF16)
    wide = pltpu.VMEM((size, channels * size), BF16)
    five = pltpu.VMEM((5,) + square, BF16)
    full = pltpu.VMEM(square, F32)
    sems = pltpu.SemaphoreType.DMA
    outs = (
        jax.ShapeDtypeStruct((1, 1) + square, F32),
        jax.ShapeDtypeStruct((1, 1) + square, BF16),
        jax.ShapeDtypeStruct((1,), F32),
    )
    made = pl.pallas_call(
        functools.partial(kernel, segs, secs),
        out_shape=outs,
        in_specs=[hbm] * 8,
        out_specs=(hbm,) * 3,
        scratch_shapes=[
            envs, envs, block, block, pltpu.VMEM((1, size), F32), block,
            pltpu.SMEM((1, 1), jnp.int32), wide, wide,
            pltpu.VMEM((size, WD * size), BF16), block, block,
            five, five, five, five,
            pltpu.VMEM((3, 16, 128), F32), pltpu.VMEM((3, secs, 16, 128), F32), block,
        ] + [full] * 12 + [
            block, pltpu.SMEM((1,), F32),
            sems((7,)), sems((3,)), sems((3,)), sems((11,)), sems((11,)), sems((10,)), sems((10,)),
            sems((3, secs)), sems((3, secs)), sems((3,)),
        ],
        compiler_params=pltpu.CompilerParams(
            collective_id=0, has_side_effects=True, vmem_limit_bytes=60 * 1024 * 1024
        ),
        cost_estimate=pl.CostEstimate(
            flops=3 * 60 * 2 * size ** 3, bytes_accessed=6 * 1024 * 1024, transcendentals=0
        ),
    )(left_env, right_env, left_piece, right_piece, guess, inverse_values, precond, sector_rows)
    vmem = pl.BlockSpec(memory_space=pltpu.VMEM)
    smem = pl.BlockSpec(memory_space=pltpu.SMEM)
    return pl.pallas_call(
        store, out_shape=outs, in_specs=[vmem, vmem, smem], out_specs=(vmem, vmem, smem)
    )(*made)


def solution(mesh):
    placed = (
        P("seg", "sec", None, None, None),
        P("seg", "sec", None, None, None),
        P("seg", "sec", None, None),
        P("seg", "sec", None, None),
        P("seg", "sec", None, None),
        P("seg", "sec", None),
        P("seg", "sec", None, None),
        P("seg", "sec"),
    )
    return jax.shard_map(
        functools.partial(shards, mesh.shape["seg"], mesh.shape["sec"]),
        mesh=mesh,
        in_specs=placed,
        out_specs=(P("seg", "sec", None, None), P("seg", "sec", None, None), P("seg")),
        check_vma=False,
    )
```

time: 62.1 us -> 52.6 us (0.85)
  Pallas kernels: 55.6 us -> 51 us
  local copies, waits for them, and re-layouts: 3.24 us -> 0 us
  between operations: 3.04 us -> 1.45 us
    pallas_call x1 -> x2, Pallas kernels: 55.6 us -> 51 us  [the longest x1 48.6 us: shards(): pl.pallas_call(functools.partial(kernel, segs, secs), out_shape=outs, in_...]
    unnamed x2 -> x0, local copies, waits for them, and re-layouts: 3.24 us -> none
where the time goes in v2:
time: 52.6 us; the launch traced here: 52.4 us
  Pallas kernels  51 us (97%)
  between operations  1.45 us (3%)
    pallas_call x1, Pallas kernels, shards(): pl.pallas_call(functools.partial(kernel, segs, secs), out_shape=outs, in_...  48.6 us
    pallas_call x1, Pallas kernels, shards(): pl.pallas_call(store, out_shape=outs, in_specs=[vmem, vmem, smem], out_sp...  2.37 us

profile of v2, /device:TPU:1, one launch (start us, length us, event | category | flops | bytes accessed | tf_op | source)
XLA Modules:
  0.0 52.4 jit_solution(6835335729124746321)
XLA Ops:
  1.3 48.6 %shard_map.103 = (f32[1,1,256,256]{3,2,1,0:T(8,128)}, bf16[1,1,256,256]{3,2,1,0:T(8,128)(2,1)}, f32[1]{0:T(128)}) custom-call(bf16[1,1,16,256,256]{4,3,2,1,0:T(8,128)(2,1)} %lenv_hbm.1, bf16[1,1,16,256,256]{4,3,2,1,0:T(8,128)(2,1)} %renv_hbm.1, bf16[1,1,256,256]{3,2,1,0:T(8,128)(2,1)} %lpiece_hbm.1, bf16[1,1,256,256]{3,2,1,0:T(8,128)(2,1)} %rpiece_hbm.1, ...), custom_call_target="tpu_custom_call" | custom-call | flops 6039797760 | bytes 6291456 | tf_op jit(solution)/shard_map/pallas_call | solution.py:450
  49.9 2.4 %shard_map.104 = (f32[1,1,256,256]{3,2,1,0:T(8,128)}, bf16[1,1,256,256]{3,2,1,0:T(8,128)(2,1)}, f32[1]{0:T(128)}) custom-call(f32[1,1,256,256]{3,2,1,0:T(8,128)} %get-tuple-element.6.polar_in, bf16[1,1,256,256]{3,2,1,0:T(8,128)(2,1)} %get-tuple-element.7.handed_in, f32[1]{0:T(128)} %get-tuple-element.8.lam_in), custom_call_target="tpu_custom_call" | custom-call | tf_op jit(solution)/shard_map/pallas_call | solution.py:475

commit v3 on v2

--- a/solution.py
+++ b/solution.py
@@ -51,7 +51,7 @@
     polar_out, handed_out, lam_out,
     lenv, renv, lpiece, guess, inv, prec, rows, inner_a, inner_b, inner_c, bnext, d_below,
     vsend, vrecv, dsend, drecv, part, gathered, wsend,
-    r_ref, g_ref, e_ref, x_ref, t_ref, h_ref, d_ref, k0_ref, k1_ref, hdg_ref, dh_ref, dt_ref, zero_ref, lam_ref,
+    r_ref, g_ref, e_ref, x_ref, t_ref, h_ref, d_ref, k0_ref, k1_ref, hdg_ref, rh_ref, dh_ref, dt_ref, zero_ref, lam_ref,
     load_sem, seg_send, seg_recv, v_send, v_recv, d_send, d_recv, ar_send, ar_recv, out_sem,
 ):
     seg = lax.axis_index("seg")
@@ -217,12 +217,13 @@
     g_ref[...] = big_g
     dg = d_ref[...] * big_g
     dh_ref[...] = dg
-    up_g = [send_up(2, top, dg[top]), send_up(2, bottom, dg[bottom])]
     put(0, 3, r_ref[...] * big_g)
     put(0, 4, e_ref[...] * big_g)
     put(0, 5, dg * dg)
     put(0, 6, dg * e_ref[...])
     ex0 = exchange(0, 8)
+    dg = dh_ref[...]
+    up_g = [send_up(2, top, dg[top]), send_up(2, bottom, dg[bottom])]
     lower(2, vsend[2], top)
     down_g = [send_down(2, top)]
     lower(2, vsend[2], bottom)
@@ -233,8 +234,12 @@
     for copy in down_e:
         copy.wait_recv()
     k0_ref[...] = together(k0_ref[...], raised, 1)
+    up_g[0].wait_recv()
+    h_ref[...] = upper_part(vrecv[2, top], top)
 
     tot = totals(0, ex0, 8)
+    up_g[1].wait_recv()
+    raised = h_ref[...] + upper_part(vrecv[2, bottom], bottom)
     n0 = tot[0:1]
     grow = 1.0 / SHRINK
     scale = 1.0 / jnp.sqrt(n0)
@@ -274,7 +279,6 @@
     put(1, 5, dt * (d * x))
     put(1, 6, dt * (d * g))
     put(1, 7, t * g)
-    raised = raised_from(2, up_g)
     for copy in down_g:
         copy.wait_recv()
     hdg = together(k1_ref[...], raised, 2) * scale_g
@@ -284,8 +288,6 @@
     g = g_ref[...]
     h = (hdg - a * hdx - s * g) * over_q
     dh = d_ref[...] * h
-    vsend[4] = dh.astype(BF16)
-    up_h = send_up(4, top, dh[top])
     h_ref[...] = h
     dh_ref[...] = dh
     d = d_ref[...]
@@ -300,6 +302,11 @@
     put(1, 14, dh * (d * x))
     put(1, 15, dh * (d * t))
     ex1 = exchange(1, 16)
+    dh = dh_ref[...]
+    vsend[4] = dh.astype(BF16)
+    up_h = send(
+        vsend.at[4, top], vrecv.at[4, top], {"sec": above}, v_send.at[8], v_recv.at[8]
+    )
     lower(4, vsend[4], bottom)
     down_h = send_down(4, bottom)
     lower(3, vsend[3], bottom)
@@ -310,6 +317,9 @@
     below_x = vrecv[0, top].astype(F32) * scale
     below_g = vrecv[2, top].astype(F32) * scale_g
     below_dt = below_d * ((below_g - (a_old * below_d + s_old) * below_x) * q_old)
+    e_ref[...] = upper_part(below_dt.astype(BF16), top)
+    up_h.wait_recv()
+    rh_ref[...] = upper_part(vrecv[4, top], top)
 
     tot = totals(1, ex1, 16)
 
@@ -332,9 +342,7 @@
     dg_dx = aa * dg_dx + ab * (tot[6:7] + tot[14:15]) + bb * tot[15:16]
     dx_dx = aa * dx_dx + 2.0 * ab * tot[5:6] + bb * tot[4:5]
     s, over_q = correction(a, x_dx, x_dg, dx_dx, dg_dx, dg_dg)
-    up_h.wait_recv()
-    fresh_below = (vrecv[4, top].astype(F32) - a * below_dt).astype(BF16)
-    raised = jnp.where(has_below, upper_part(fresh_below, top), 0.0)
+    raised = jnp.where(has_below, rh_ref[...] - a * e_ref[...], 0.0)
     x = al * x_ref[...] + be * t_ref[...]
     g = al * g_ref[...] + be * h_ref[...]
     fresh = be * (dh_ref[...] - a * dt_ref[...])
@@ -378,10 +386,10 @@
     turned = split(al * g_ref[...] + be * h_ref[...])
     gram = (aa * k0_ref[...] + ab * k1_ref[...] + bb * e_ref[...]) * (over * over)
     for step in range(NS_STEPS):
-        pair = split(polar)
+        near = polar.astype(BF16)
         if step:
-            gram = three(nt, pair, pair)
-        polar = 1.5 * polar - 0.5 * three(nn, split(gram), pair)
+            gram = nt(near, near)
+        polar = 1.5 * polar - 0.5 * nn(gram.astype(BF16), near)
     r_ref[...] = polar
     polar_copy = pltpu.make_async_copy(r_ref, polar_out.at[0, 0], out_sem.at[0])
     polar_copy.start()
@@ -458,7 +466,7 @@
             pltpu.VMEM((size, WD * size), BF16), block, block,
             five, five, five, five,
             pltpu.VMEM((3, 16, 128), F32), pltpu.VMEM((3, secs, 16, 128), F32), block,
-        ] + [full] * 12 + [
+        ] + [full] * 13 + [
             block, pltpu.SMEM((1,), F32),
             sems((7,)), sems((3,)), sems((3,)), sems((11,)), sems((11,)), sems((10,)), sems((10,)),
             sems((3, secs)), sems((3, secs)), sems((3,)),

time: 52.6 us -> 51.9 us (0.987)
  Pallas kernels: 51 us -> 50.3 us
    pallas_call x1, Pallas kernels: 48.6 us -> 47.9 us  [shards(): pl.pallas_call(functools.partial(kernel, segs, secs), out_shape=outs, in_...]
where the time goes in v3:
time: 51.9 us; the launch traced here: 51.7 us
  Pallas kernels  50.3 us (97%)
  between operations  1.45 us (3%)
    pallas_call x1, Pallas kernels, shards(): pl.pallas_call(functools.partial(kernel, segs, secs), out_shape=outs, in_...  47.9 us
    pallas_call x1, Pallas kernels, shards(): pl.pallas_call(store, out_shape=outs, in_specs=[vmem, vmem, smem], out_sp...  2.37 us

profile of v3, /device:TPU:1, one launch (start us, length us, event | category | flops | bytes accessed | tf_op | source)
XLA Modules:
  0.0 51.7 jit_solution(2145312027954532071)
XLA Ops:
  1.3 47.9 %shard_map.103 = (f32[1,1,256,256]{3,2,1,0:T(8,128)}, bf16[1,1,256,256]{3,2,1,0:T(8,128)(2,1)}, f32[1]{0:T(128)}) custom-call(bf16[1,1,16,256,256]{4,3,2,1,0:T(8,128)(2,1)} %lenv_hbm.1, bf16[1,1,16,256,256]{4,3,2,1,0:T(8,128)(2,1)} %renv_hbm.1, bf16[1,1,256,256]{3,2,1,0:T(8,128)(2,1)} %lpiece_hbm.1, bf16[1,1,256,256]{3,2,1,0:T(8,128)(2,1)} %rpiece_hbm.1, ...), custom_call_target="tpu_custom_call" | custom-call | flops 6039797760 | bytes 6291456 | tf_op jit(solution)/shard_map/pallas_call | solution.py:458
  49.2 2.4 %shard_map.104 = (f32[1,1,256,256]{3,2,1,0:T(8,128)}, bf16[1,1,256,256]{3,2,1,0:T(8,128)(2,1)}, f32[1]{0:T(128)}) custom-call(f32[1,1,256,256]{3,2,1,0:T(8,128)} %get-tuple-element.6.polar_in, bf16[1,1,256,256]{3,2,1,0:T(8,128)(2,1)} %get-tuple-element.7.handed_in, f32[1]{0:T(128)} %get-tuple-element.8.lam_in), custom_call_target="tpu_custom_call" | custom-call | tf_op jit(solution)/shard_map/pallas_call | solution.py:483

commit v4 on v3

--- a/solution.py
+++ b/solution.py
@@ -285,6 +285,8 @@
     hdx = k0_ref[...] * scale
     hdg_ref[...] = hdg
     k0_ref[...] = hdx
+    lower(3, vsend[3], bottom)
+    r_ref[...] = diagonal(vsend[3])
     g = g_ref[...]
     h = (hdg - a * hdx - s * g) * over_q
     dh = d_ref[...] * h
@@ -309,10 +311,8 @@
     )
     lower(4, vsend[4], bottom)
     down_h = send_down(4, bottom)
-    lower(3, vsend[3], bottom)
     down_t = send_down(3, bottom)
     k1_ref[...] = diagonal(vsend[4])
-    r_ref[...] = diagonal(vsend[3])
     below_d = d_below[top].astype(F32)
     below_x = vrecv[0, top].astype(F32) * scale
     below_g = vrecv[2, top].astype(F32) * scale_g
@@ -433,10 +433,23 @@
             hand.wait_recv()
 
 
-def store(polar_in, handed_in, lam_in, polar_out, handed_out, lam_out):
-    polar_out[...] = polar_in[...]
-    handed_out[...] = handed_in[...]
-    lam_out[0] = lam_in[0]
+def store(polar_in, handed_in, lam_in, polar_out, handed_out, lam_out, polar, handed, lam, sem):
+    half = polar.shape[0] // 2
+    ways = [
+        (polar_in.at[0, 0, :half], polar.at[:half], polar_out.at[0, 0, :half]),
+        (polar_in.at[0, 0, half:], polar.at[half:], polar_out.at[0, 0, half:]),
+        (handed_in.at[0, 0], handed, handed_out.at[0, 0]),
+        (lam_in, lam, lam_out),
+    ]
+    ins = [pltpu.make_async_copy(a, b, sem.at[0, n]) for n, (a, b, _) in enumerate(ways)]
+    outs = [pltpu.make_async_copy(b, c, sem.at[1, n]) for n, (_, b, c) in enumerate(ways)]
+    for copy in ins:
+        copy.start()
+    for first, second in zip(ins, outs):
+        first.wait()
+        second.start()
+    for copy in outs:
+        copy.wait()
 
 
 def shards(segs, secs, left_env, right_env, left_piece, right_piece, guess, inverse_values,
@@ -478,10 +491,10 @@
             flops=3 * 60 * 2 * size ** 3, bytes_accessed=6 * 1024 * 1024, transcendentals=0
         ),
     )(left_env, right_env, left_piece, right_piece, guess, inverse_values, precond, sector_rows)
-    vmem = pl.BlockSpec(memory_space=pltpu.VMEM)
-    smem = pl.BlockSpec(memory_space=pltpu.SMEM)
     return pl.pallas_call(
-        store, out_shape=outs, in_specs=[vmem, vmem, smem], out_specs=(vmem, vmem, smem)
+        store, out_shape=outs, in_specs=[hbm] * 3, out_specs=(hbm,) * 3,
+        scratch_shapes=[full, block, pltpu.SMEM((1,), F32), sems((2, 4))],
+        compiler_params=pltpu.CompilerParams(vmem_limit_bytes=60 * 1024 * 1024),
     )(*made)
 
 

time: 51.9 us -> 52.1 us (level)
  no operation moved by 1% of the time
where the time goes in v4:
time: 52.1 us; the launch traced here: 51.9 us
  Pallas kernels  50.5 us (97%)
  between operations  1.45 us (3%)
    pallas_call x1, Pallas kernels, shards(): pl.pallas_call(functools.partial(kernel, segs, secs), out_shape=outs, in_...  48.1 us
    pallas_call x1, Pallas kernels, shards(): pl.pallas_call(store, out_shape=outs, in_specs=[hbm] * 3, out_specs=(hbm,...  2.39 us

profile of v4, /device:TPU:1, one launch (start us, length us, event | category | flops | bytes accessed | tf_op | source)
XLA Modules:
  0.0 51.9 jit_solution(3611464734526894972)
XLA Ops:
  1.3 48.1 %shard_map.103 = (f32[1,1,256,256]{3,2,1,0:T(8,128)}, bf16[1,1,256,256]{3,2,1,0:T(8,128)(2,1)}, f32[1]{0:T(128)}) custom-call(bf16[1,1,16,256,256]{4,3,2,1,0:T(8,128)(2,1)} %lenv_hbm.1, bf16[1,1,16,256,256]{4,3,2,1,0:T(8,128)(2,1)} %renv_hbm.1, bf16[1,1,256,256]{3,2,1,0:T(8,128)(2,1)} %lpiece_hbm.1, bf16[1,1,256,256]{3,2,1,0:T(8,128)(2,1)} %rpiece_hbm.1, ...), custom_call_target="tpu_custom_call" | custom-call | flops 6039797760 | bytes 6291456 | tf_op jit(solution)/shard_map/pallas_call | solution.py:471
  49.4 2.4 %shard_map.104 = (f32[1,1,256,256]{3,2,1,0:T(8,128)}, bf16[1,1,256,256]{3,2,1,0:T(8,128)(2,1)}, f32[1]{0:T(128)}) custom-call(f32[1,1,256,256]{3,2,1,0:T(8,128)} %get-tuple-element.6.polar_in, bf16[1,1,256,256]{3,2,1,0:T(8,128)(2,1)} %get-tuple-element.7.handed_in, f32[1]{0:T(128)} %get-tuple-element.8.lam_in), custom_call_target="tpu_custom_call" | custom-call | tf_op jit(solution)/shard_map/pallas_call | solution.py:494
